TPU v7x, 128 devices: a whole 4x4x4 slice. The times are simulated.
128 devices in a mesh: row: 16 (over z_lo, y, core), col: 8 (over z_hi, x).
Axes of the slice: x: 4, y: 4, z: 4 (z_hi: 2, z_lo: 2; z = z_hi * 2 + z_lo), core: 2. Of those that a mesh axis runs over, the one named last changes fastest.
Arguments:
- a_tiles: bfloat16 [2048, 32, 64, 64], P('row', 'col'), may hold values from -6 to 6
- a_cols: int32 [2048, 32], P('row', 'col'), may hold values from 0 to 2047, as said below
- p_tiles: bfloat16 [2048, 64, 64], P(('col', 'row')), may hold values from -0.75 to 0.75
- agg_sizes: int32 [16, 16], P('row'), may hold values from 1 to 24, 128 in all within a row
Outputs:
- coarse: float32 [256, 64, 16384], P(None, None, ('col', 'row'))
Inputs may be any that keep to these rules, and one draw needn't show every extreme that they name: a_cols[i, s] is a fine block of column group s // 4: from (s // 4) * 256 to (s // 4 + 1) * 256 - 1.
All inputs are finite; a program needn't handle non-finite values.
Results may differ from a plain program's by a relative error of at most 0.0029.
Values may be sent and summed in bfloat16 or wider, within the bound.
A program may use at most 192 MiB of HBM per device.

v0:
```python
import functools

import jax
import jax.numpy as jnp
from jax import lax
from jax.experimental import pallas as pl
from jax.experimental.pallas import tpu as pltpu
from jax.sharding import PartitionSpec as P

MESH = pl.DeviceIdType.MESH
ROWS = 16
COLS = 8
MIB = 1 << 20


def spread_kernel(p_ref, s_ref, col_out, row_out, mine, send_sem, col_sem, row_sem, local_sem):
    row = lax.axis_index("row")
    col = lax.axis_index("col")
    owner = (2 * col + row // 8) % ROWS
    barrier = pltpu.get_barrier_semaphore()

    @pl.loop(1, ROWS)
    def _(step):
        pl.semaphore_signal(barrier, 1, device_id=((row + step) % ROWS, col), device_id_type=MESH)

    @pl.loop(0, 8)
    def _(step):
        src = (8 * (row % 2) + step, row // 2)

        @pl.when(jnp.logical_or(src[0] != row, src[1] != col))
        def _():
            pl.semaphore_signal(barrier, 1, device_id=src, device_id_type=MESH)

    for k in range(8):
        mine[pl.ds(64 * k, 64), :] = jnp.concatenate([p_ref[2 * k], p_ref[2 * k + 1]], axis=-1)
    mine[pl.ds(512, 16), :] = s_ref[...]
    self_send = jnp.logical_and(row == owner, True)
    pl.semaphore_wait(barrier, ROWS - 1 + 8 - jnp.where(self_send, 1, 0))

    own = pltpu.make_async_copy(mine, col_out.at[row], local_sem.at[0])
    own.start()

    def col_copy(step):
        return pltpu.make_async_remote_copy(
            src_ref=mine,
            dst_ref=col_out.at[row],
            send_sem=send_sem.at[step],
            recv_sem=col_sem.at[row],
            device_id=((row + step) % ROWS, col),
            device_id_type=MESH,
        )

    def row_copy(step):
        return pltpu.make_async_remote_copy(
            src_ref=mine.at[pl.ds(0, 512)],
            dst_ref=row_out.at[row % 8],
            send_sem=send_sem.at[ROWS + step],
            recv_sem=row_sem.at[row % 8],
            device_id=(owner, (col + step) % COLS),
            device_id_type=MESH,
        )

    def row_local():
        return pltpu.make_async_copy(mine.at[pl.ds(0, 512)], row_out.at[row % 8], local_sem.at[1])

    @pl.loop(1, ROWS)
    def _(step):
        col_copy(step).start()

    @pl.when(self_send)
    def _():
        row_local().start()

    @pl.when(jnp.logical_not(self_send))
    def _():
        row_copy(0).start()

    @pl.loop(1, COLS)
    def _(step):
        row_copy(step).start()

    own.wait()

    @pl.when(self_send)
    def _():
        row_local().wait()

    @pl.when(jnp.logical_not(self_send))
    def _():
        row_copy(0).wait_send()

    @pl.loop(1, COLS)
    def _(step):
        row_copy(step).wait_send()

    @pl.loop(1, ROWS)
    def _(step):
        col_copy(step).wait_send()
        src = (row + step) % ROWS
        pltpu.make_async_copy(col_out.at[src], col_out.at[src], col_sem.at[src]).wait()

    @pl.loop(0, 8)
    def _(step):
        src = (8 * (row % 2) + step, row // 2)

        @pl.when(jnp.logical_or(src[0] != row, src[1] != col))
        def _():
            pltpu.make_async_copy(row_out.at[step], row_out.at[step], row_sem.at[step]).wait()


def spread(p_tiles, sizes):
    return pl.pallas_call(
        spread_kernel,
        out_shape=(
            jax.ShapeDtypeStruct((ROWS, 528, 128), jnp.bfloat16),
            jax.ShapeDtypeStruct((8, 512, 128), jnp.bfloat16),
        ),
        in_specs=[pl.BlockSpec(memory_space=pltpu.VMEM)] * 2,
        out_specs=[pl.BlockSpec(memory_space=pl.ANY)] * 2,
        scratch_shapes=[
            pltpu.VMEM((528, 128), jnp.bfloat16),
            pltpu.SemaphoreType.DMA((ROWS + COLS,)),
            pltpu.SemaphoreType.DMA((ROWS,)),
            pltpu.SemaphoreType.DMA((8,)),
            pltpu.SemaphoreType.DMA((2,)),
        ],
        compiler_params=pltpu.CompilerParams(collective_id=0, has_side_effects=True),
    )(p_tiles, sizes)


CHUNK = 16


def blocks_kernel(cols_ref, mine_ref, sizes_ref, a_hbm, col_ref, row_ref, out_hbm,
                  a_buf, table, left, acc, out_buf, bmap, amap, a_sem, out_sem):
    chunks = 128 // CHUNK

    def a_copy(k):
        return pltpu.make_async_copy(
            a_hbm.at[pl.ds(CHUNK * k, CHUNK)], a_buf.at[pl.ds(CHUNK * k, CHUNK)], a_sem.at[k]
        )

    for k in range(chunks):
        a_copy(k).start()

    @pl.loop(0, 256, unroll=8)
    def _(k):
        acc[pl.ds(64 * k, 64), :] = jnp.zeros((64, 128), jnp.float32)

    def walk(total, size_of, put):
        def step(f, state):
            at, end = state
            go = f >= end
            at = jnp.where(go, at + 1, at)
            end = jnp.where(go, end + size_of(jnp.minimum(at, 31)), end)
            put(f, at)
            return at, end

        lax.fori_loop(0, total, step, (jnp.int32(0), size_of(0)))

    def put_b(f, at):
        bmap[f] = at

    def put_a(f, at):
        amap[f] = at

    walk(256, lambda k: sizes_ref[k // 16, k % 16], put_b)
    walk(128, lambda k: mine_ref[0, k % 16], put_a)

    lane = lax.broadcasted_iota(jnp.int32, (64, 128), 1)
    zero = jnp.zeros((64, 128), jnp.bfloat16)

    @pl.loop(0, 128, unroll=2)
    def _(k):
        pair = col_ref[k // 8, pl.ds(pl.multiple_of(64 * (k % 8), 64), 64), :]
        turned = jnp.concatenate([pair[:, 64:], pair[:, :64]], axis=-1)
        right0 = bmap[2 * k] % 2
        right1 = bmap[2 * k + 1] % 2
        keep0 = (lane // 64) == right0
        keep1 = (lane // 64) == right1
        first = jnp.where(right0 == 0, pair, turned)
        second = jnp.where(right1 == 0, turned, pair)
        table[2 * k] = jnp.where(keep0, first, zero)
        table[2 * k + 1] = jnp.where(keep1, second, zero)
        own = row_ref[k // 16, pl.ds(pl.multiple_of(64 * (k % 8), 64), 64), :] if False else None

    @pl.loop(0, 64, unroll=2)
    def _(k):
        own = row_ref[k // 8, pl.ds(pl.multiple_of(64 * (k % 8), 64), 64), :]
        left[k] = own.T

    base = lax.axis_index("col") * 256
    group = 4

    @pl.loop(0, chunks)
    def _(chunk):
        a_copy(chunk).wait()

        @pl.loop(0, CHUNK // group)
        def _(step):
            first = chunk * CHUNK + step * group
            products = []
            for r in range(group):
                row = []
                for s in range(4):
                    j = cols_ref[first + r, s] - base
                    row.append(
                        jnp.dot(
                            a_buf[first + r, s], table[j], preferred_element_type=jnp.float32
                        ).astype(jnp.bfloat16)
                    )
                products.append(row)
            pieces = []
            for r in range(group):
                i = first + r
                pt = left[i // 2, pl.ds(pl.multiple_of(64 * (r % 2), 64), 64), :]
                pieces.append(
                    jnp.dot(pt, jnp.concatenate(products[r], axis=-1), preferred_element_type=jnp.float32)
                )
            for r in range(group):
                i = first + r
                a = amap[i]
                for s in range(4):
                    b = bmap[cols_ref[i, s] - base]
                    at = pl.multiple_of(((b // 2) * 16 + a) * 64, 64)
                    acc[pl.ds(at, 64), :] += pieces[r][:, 128 * s:128 * s + 128]

    for d in range(ROWS):
        out_buf[d] = acc[pl.ds(1024 * d, 1024), :].astype(jnp.bfloat16)
        pltpu.make_async_copy(out_buf.at[d], out_hbm.at[d], out_sem.at[d]).start()
    for d in range(ROWS):
        pltpu.make_async_copy(out_buf.at[d], out_hbm.at[d], out_sem.at[d]).wait()


def blocks(a_cols, mine, sizes, a_tiles, col_p, row_p):
    smem = pl.BlockSpec(memory_space=pltpu.SMEM)
    vmem = pl.BlockSpec(memory_space=pltpu.VMEM)
    hbm = pl.BlockSpec(memory_space=pl.ANY)
    return pl.pallas_call(
        blocks_kernel,
        out_shape=jax.ShapeDtypeStruct((ROWS, 1024, 128), jnp.bfloat16),
        in_specs=[smem, smem, smem, hbm, vmem, vmem],
        out_specs=hbm,
        scratch_shapes=[
            pltpu.VMEM((128, 4, 64, 64), jnp.bfloat16),
            pltpu.VMEM((256, 64, 128), jnp.bfloat16),
            pltpu.VMEM((64, 128, 64), jnp.bfloat16),
            pltpu.VMEM((ROWS * 1024, 128), jnp.float32),
            pltpu.VMEM((ROWS, 1024, 128), jnp.bfloat16),
            pltpu.SMEM((256,), jnp.int32),
            pltpu.SMEM((128,), jnp.int32),
            pltpu.SemaphoreType.DMA((128 // CHUNK,)),
            pltpu.SemaphoreType.DMA((ROWS,)),
        ],
        compiler_params=pltpu.CompilerParams(vmem_limit_bytes=56 * MIB),
    )(a_cols, mine, sizes, a_tiles, col_p, row_p)


def exchange_kernel(src_ref, out_ref, send_sem, recv_sem, local_sem):
    row = lax.axis_index("row")
    col = lax.axis_index("col")
    barrier = pltpu.get_barrier_semaphore()

    @pl.loop(1, ROWS)
    def _(step):
        pl.semaphore_signal(barrier, 1, device_id=((row + step) % ROWS, col), device_id_type=MESH)

    pl.semaphore_wait(barrier, ROWS - 1)
    own = pltpu.make_async_copy(src_ref.at[row], out_ref.at[row], local_sem)
    own.start()

    def copy(step):
        to = (row + step) % ROWS
        return pltpu.make_async_remote_copy(
            src_ref=src_ref.at[to],
            dst_ref=out_ref.at[row],
            send_sem=send_sem.at[step],
            recv_sem=recv_sem.at[row],
            device_id=(to, col),
            device_id_type=MESH,
        )

    @pl.loop(1, ROWS)
    def _(step):
        copy(step).start()

    own.wait()

    @pl.loop(1, ROWS)
    def _(step):
        copy(step).wait_send()
        src = (row + step) % ROWS
        pltpu.make_async_copy(out_ref.at[src], out_ref.at[src], recv_sem.at[src]).wait()


def exchange(parts):
    return pl.pallas_call(
        exchange_kernel,
        out_shape=jax.ShapeDtypeStruct(parts.shape, parts.dtype),
        in_specs=[pl.BlockSpec(memory_space=pl.ANY)],
        out_specs=pl.BlockSpec(memory_space=pl.ANY),
        scratch_shapes=[
            pltpu.SemaphoreType.DMA((ROWS,)),
            pltpu.SemaphoreType.DMA((ROWS,)),
            pltpu.SemaphoreType.DMA,
        ],
        compiler_params=pltpu.CompilerParams(collective_id=1, has_side_effects=True),
    )(parts)


def per_device(a_tiles, a_cols, p_tiles, agg_sizes):
    col = lax.axis_index("col")
    sizes = jnp.zeros((16, 128), jnp.bfloat16).at[0, :16].set(agg_sizes[0].astype(jnp.bfloat16))
    col_p, row_p = spread(p_tiles, sizes)
    col_sizes = lax.dynamic_slice(col_p, (2 * col, 512, 0), (2, 1, 16))[:, 0, :].astype(jnp.int32)
    parts = blocks(a_cols, agg_sizes, col_sizes, a_tiles, col_p, row_p)
    got = exchange(parts)
    return got.reshape(256, 64, 128).astype(jnp.float32)


def solution(mesh):
    return jax.shard_map(
        per_device,
        mesh=mesh,
        in_specs=(
            P("row", "col", None, None),
            P("row", "col"),
            P(("col", "row"), None, None),
            P("row", None),
        ),
        out_specs=P(None, None, ("col", "row")),
        check_vma=False,
    )
```

profile of v0, /device:TPU:5, one launch (start us, length us, event | category | flops | bytes accessed | tf_op | source)
XLA Modules:
  0.0 193.0 jit_solution(11448380262618312894)
XLA Ops:
  0.0 0.7 convert_element_type.15
  0.7 0.6 scatter.4.s_ref
  1.3 1.4 copy.5.cols_ref
  2.7 62.4 %shard_map.46 = (bf16[16,528,128]{2,1,0:T(8,128)(2,1)}, bf16[8,512,128]{2,1,0:T(8,128)(2,1)}) custom-call(bf16[16,64,64]{2,1,0:T(8,128)(2,1)} %p_ref.1, bf16[16,128]{1,0:T(8,128)(2,1)} %scatter.4.s_ref), custom_call_target="tpu_custom_call" | custom-call | tf_op jit(solution)/shard_map/pallas_call | solution.py:112
  65.1 1.3 dynamic-slice_convert_fusion
  66.4 12.9 %copy.6.a_hbm = bf16[128,4,64,64]{3,2,1,0:T(8,128)(2,1)} copy(bf16[128,4,64,64]{0,3,2,1:T(8,128)(2,1)} %param.6) | data formatting | bytes 8388608 | tf_op args[0]
  79.3 30.4 %shard_map.47.src_ref = bf16[16,1024,128]{2,1,0:T(8,128)(2,1)} custom-call(s32[128,4]{1,0:T(8,128)} %copy.5.cols_ref, s32[1,16]{1,0:T(1,128)} %mine_ref.1, s32[2,16]{1,0:T(2,128)} %bitcast.4, bf16[128,4,64,64]{3,2,1,0:T(8,128)(2,1)} %copy.6.a_hbm, bf16[16,528,128]{2,1,0:T(8,128)(2,1)} %get-tuple-element.19.col_ref, ...), custom_call_target="tpu_custom_call" | custom-call | tf_op jit(solution)/shard_map/pallas_call | solution.py:239
  109.7 76.7 %shard_map.48 = bf16[16,1024,128]{2,1,0:T(8,128)(2,1)} custom-call(bf16[16,1024,128]{2,1,0:T(8,128)(2,1)} %shard_map.47.src_ref), custom_call_target="tpu_custom_call" | custom-call | tf_op jit(solution)/shard_map/pallas_call | solution.py:297
  186.4 6.6 %convert.2 = f32[256,64,128]{2,1,0:T(8,128)} convert(bf16[256,64,128]{2,1,0:T(8,128)(2,1)} %bitcast.3) | non-fusion elementwise | flops 2097152 | bytes 12582912 | tf_op jit(solution)/shard_map/convert_element_type | solution.py:318
where the time goes:
time: 193 us
  Pallas kernels  170 us (88%)
  local copies, waits for them, and re-layouts  14.9 us (8%)
  other arithmetic  8.54 us (4%)
    pallas_call x1, Pallas kernels, exchange(): pl.pallas_call(exchange_kernel, out_shape=jax.ShapeDtypeStruct(parts.shap...  76.7 us
    pallas_call x1, Pallas kernels, spread(): pl.pallas_call(spread_kernel, out_shape=(jax.ShapeDtypeStruct((ROWS, 528,...  62.4 us
    pallas_call x1, Pallas kernels, blocks(): pl.pallas_call(blocks_kernel, out_shape=jax.ShapeDtypeStruct((ROWS, 1024,...  30.4 us
    unnamed x2, local copies, waits for them, and re-layouts  14.3 us
    convert_element_type x1, other arithmetic, per_device(): return got.reshape(256, 64, 128).astype(jnp.float32)  6.63 us

commit v1 on v0

v1 whole, which is shorter than its diff:
```python
import jax
import jax.numpy as jnp
from jax import lax
from jax.experimental import pallas as pl
from jax.experimental.pallas import tpu as pltpu
from jax.sharding import PartitionSpec as P

MESH = pl.DeviceIdType.MESH
ROWS = 16
COLS = 8
MIB = 1 << 20
PITCH = 136
BF = jnp.bfloat16
F32 = jnp.float32


def place(zl, y, core, zh, x):
    return (zl * 8 + y * 2 + core, zh * 4 + x)


def spread_kernel(p_ref, s_ref, a_hbm, col_out, row_out, a_out,
                  mine, pad, a_in, mid, a_buf,
                  send_sem, col_sem, row_sem, local_sem, a_sem, out_sem):
    row = lax.axis_index("row")
    col = lax.axis_index("col")
    zl, y, core = row // 8, (row // 2) % 4, row % 2
    zh, x = col // 4, col % 4

    sibling = place(zl, y, 1 - core, zh, x)
    partner = place(1 - zl, y, core, zh, x)
    along_y = [place(zl, (y + d) % 4, core, zh, x) for d in (1, 3, 2)]
    across = place(zl, y, core, 1 - zh, x)
    along_x = [place(zl, y, core, zh, (x + d) % 4) for d in (1, 3, 2)]
    to = place(zh, x, zl, core, y)
    source = place(core, x, zh, zl, y)
    stays = jnp.logical_and(to[0] == row, to[1] == col)
    moves = jnp.logical_not(stays)

    for k in range(8):
        a_copy = pltpu.make_async_copy(
            a_hbm.at[:, pl.ds(8 * k, 8)], a_in.at[:, pl.ds(8 * k, 8)], a_sem.at[k]
        )
        a_copy.start()

    barrier = pltpu.get_barrier_semaphore()
    for there in [sibling, partner, *along_y, across, *along_x]:
        pl.semaphore_signal(barrier, 1, device_id=there, device_id_type=MESH)

    @pl.when(moves)
    def _():
        pl.semaphore_signal(barrier, 1, device_id=source, device_id_type=MESH)

    for k in range(8):
        mine[pl.ds(64 * k, 64), :] = jnp.concatenate([p_ref[2 * k], p_ref[2 * k + 1]], axis=-1)
    pad[...] = jnp.zeros_like(pad)
    pad[0:1, 0:16] = s_ref[...].astype(F32)
    mine[pl.ds(512, 16), :] = pad[...].astype(BF)

    pl.semaphore_wait(barrier, 9 + jnp.where(stays, 0, 1))

    count = [0]
    sent = []

    def send(src, dst, sem, there):
        k = count[0]
        count[0] += 1
        copy = pltpu.make_async_remote_copy(
            src_ref=src, dst_ref=dst, send_sem=send_sem.at[k], recv_sem=sem,
            device_id=there, device_id_type=MESH,
        )
        copy.start()
        sent.append(copy)

    def col_slot(index):
        return col_out.at[index]

    def arrived(ref, sem):
        pltpu.make_async_copy(ref, ref, sem).wait()

    def row_of(a, b, c):
        return a * 8 + b * 2 + c

    held = 2 * x + zh
    first = pltpu.make_async_remote_copy(
        src_ref=mine.at[pl.ds(0, 512)], dst_ref=row_out.at[2 * y + core],
        send_sem=send_sem.at[24], recv_sem=row_sem.at[2 * y + core],
        device_id=to, device_id_type=MESH,
    )
    first_here = pltpu.make_async_copy(
        mine.at[pl.ds(0, 512)], row_out.at[2 * y + core], row_sem.at[2 * y + core]
    )

    @pl.when(moves)
    def _():
        first.start()

    @pl.when(stays)
    def _():
        first_here.start()

    for there in [partner, *along_y, sibling]:
        send(mine, col_slot(row), col_sem.at[row], there)
    own = pltpu.make_async_copy(mine, col_slot(row), local_sem)
    own.start()

    eye = (
        lax.broadcasted_iota(jnp.int32, (128, 128), 0)
        == lax.broadcasted_iota(jnp.int32, (128, 128), 1)
    ).astype(BF)

    def turn(k):
        pltpu.make_async_copy(
            a_hbm.at[:, pl.ds(8 * k, 8)], a_in.at[:, pl.ds(8 * k, 8)], a_sem.at[k]
        ).wait()

        @pl.loop(0, 8)
        def _(n):
            u = 8 * k + n
            wide = jnp.concatenate([a_in[s, u] for s in range(4)], axis=0)
            tiles = lax.dot_general(eye, wide, (((1,), (1,)), ((), ())), preferred_element_type=F32)
            for h in range(2):
                mid[h, pl.ds(pl.multiple_of(PITCH * u, 8), 128), :] = tiles[:, 128 * h:128 * h + 128]

    def pick(k):
        @pl.loop(0, 32)
        def _(n):
            i = 32 * k + n
            for h in range(2):
                a_buf[i, :, 128 * h:128 * h + 128] = mid[h, pl.ds(i, 64, stride=PITCH), :].astype(BF)

        pltpu.make_async_copy(
            a_buf.at[pl.ds(32 * k, 32)], a_out.at[pl.ds(32 * k, 32)], out_sem.at[k]
        ).start()

    turn(0)
    turn(1)

    other = row_of(1 - zl, y, core)
    arrived(col_slot(other), col_sem.at[other])
    for there in [*along_y, sibling]:
        send(col_slot(other), col_slot(other), col_sem.at[other], there)
    arrived(row_out.at[held], row_sem.at[held])
    for there in [across, *along_x]:
        send(row_out.at[held], row_out.at[held], row_sem.at[held], there)

    turn(2)
    turn(3)

    across_held = 2 * x + 1 - zh
    arrived(row_out.at[across_held], row_sem.at[across_held])
    for there in along_x:
        send(row_out.at[across_held], row_out.at[across_held], row_sem.at[across_held], there)

    turn(4)
    turn(5)
    for d in (1, 3, 2):
        index = row_of(zl, (y + d) % 4, core)
        arrived(col_slot(index), col_sem.at[index])
        send(col_slot(index), col_slot(index), col_sem.at[index], sibling)
    turn(6)
    turn(7)
    pick(0)
    pick(1)
    for d in (1, 3, 2):
        index = row_of(1 - zl, (y + d) % 4, core)
        arrived(col_slot(index), col_sem.at[index])
        send(col_slot(index), col_slot(index), col_sem.at[index], sibling)
    pick(2)
    pick(3)

    own.wait()
    for a in (0, 1):
        for b in range(4):
            index = row_of(a, b, 1 - core)
            arrived(col_slot(index), col_sem.at[index])
    for d in (1, 3, 2):
        for h in (0, 1):
            index = 2 * ((x + d) % 4) + h
            arrived(row_out.at[index], row_sem.at[index])

    @pl.when(moves)
    def _():
        first.wait_send()

    for copy in sent:
        copy.wait_send()
    for k in range(4):
        pltpu.make_async_copy(
            a_buf.at[pl.ds(32 * k, 32)], a_out.at[pl.ds(32 * k, 32)], out_sem.at[k]
        ).wait()


def spread(p_tiles, sizes, a_turned):
    vmem = pl.BlockSpec(memory_space=pltpu.VMEM)
    hbm = pl.BlockSpec(memory_space=pl.ANY)
    return pl.pallas_call(
        spread_kernel,
        out_shape=(
            jax.ShapeDtypeStruct((ROWS, 528, 128), BF),
            jax.ShapeDtypeStruct((8, 512, 128), BF),
            jax.ShapeDtypeStruct((128, 64, 256), BF),
        ),
        in_specs=[vmem, vmem, hbm],
        out_specs=[hbm] * 3,
        scratch_shapes=[
            pltpu.VMEM((528, 128), BF),
            pltpu.VMEM((16, 128), F32),
            pltpu.VMEM((4, 64, 64, 128), BF),
            pltpu.VMEM((2, 64 * PITCH, 128), F32),
            pltpu.VMEM((128, 64, 256), BF),
            pltpu.SemaphoreType.DMA((25,)),
            pltpu.SemaphoreType.DMA((ROWS,)),
            pltpu.SemaphoreType.DMA((8,)),
            pltpu.SemaphoreType.DMA,
            pltpu.SemaphoreType.DMA((8,)),
            pltpu.SemaphoreType.DMA((4,)),
        ],
        compiler_params=pltpu.CompilerParams(
            collective_id=0, has_side_effects=True, vmem_limit_bytes=24 * MIB
        ),
    )(p_tiles, sizes, a_turned)


CHUNK = 16


def blocks_kernel(cols_ref, a_hbm, col_ref, row_ref, out_hbm,
                  a_buf, table, left, acc, out_buf, maps, smaps, a_sem, out_sem, map_sem):
    chunks = 128 // CHUNK
    row = lax.axis_index("row")
    col = lax.axis_index("col")

    def a_copy(k):
        return pltpu.make_async_copy(
            a_hbm.at[pl.ds(CHUNK * k, CHUNK)], a_buf.at[pl.ds(CHUNK * k, CHUNK)], a_sem.at[k]
        )

    for k in range(chunks):
        a_copy(k).start()

    lower = (
        lax.broadcasted_iota(jnp.int32, (16, 128), 1) <= lax.broadcasted_iota(jnp.int32, (16, 128), 0)
    )
    fine = lax.broadcasted_iota(jnp.int32, (16, 128), 1).astype(F32)

    def aggregates(index):
        sizes = col_ref[index, pl.ds(512, 16), :].astype(F32)[0:1, :]
        ends = jnp.sum(jnp.where(lower, sizes, 0.0), axis=1, keepdims=True)
        return jnp.sum(jnp.where(ends <= fine, 1.0, 0.0), axis=0, keepdims=True).astype(jnp.int32)

    maps[0:1, :] = aggregates(2 * col)
    maps[1:2, :] = aggregates(2 * col + 1) + 16
    maps[2:3, :] = aggregates(row)
    to_smem = pltpu.make_async_copy(maps, smaps, map_sem)
    to_smem.start()

    @pl.loop(0, 256, unroll=8)
    def _(k):
        acc[pl.ds(64 * k, 64), :] = jnp.zeros((64, 128), F32)

    @pl.loop(0, 64, unroll=2)
    def _(k):
        own = row_ref[k // 8, pl.ds(pl.multiple_of(64 * (k % 8), 64), 64), :]
        left[k] = own.T

    lane = lax.broadcasted_iota(jnp.int32, (64, 128), 1)
    zero = jnp.zeros((64, 128), BF)
    to_smem.wait()

    @pl.loop(0, 128, unroll=2)
    def _(k):
        pair = col_ref[k // 8, pl.ds(pl.multiple_of(64 * (k % 8), 64), 64), :]
        turned = jnp.concatenate([pair[:, 64:], pair[:, :64]], axis=-1)
        right0 = smaps[k // 64, 2 * (k % 64)] % 2
        right1 = smaps[k // 64, 2 * (k % 64) + 1] % 2
        keep0 = (lane // 64) == right0
        keep1 = (lane // 64) == right1
        first = jnp.where(right0 == 0, pair, turned)
        second = jnp.where(right1 == 0, turned, pair)
        table[2 * k] = jnp.where(keep0, first, zero)
        table[2 * k + 1] = jnp.where(keep1, second, zero)

    base = col * 256
    group = 4

    @pl.loop(0, chunks)
    def _(chunk):
        a_copy(chunk).wait()

        @pl.loop(0, CHUNK // group)
        def _(step):
            first = chunk * CHUNK + step * group
            products = []
            for r in range(group):
                for h in range(2):
                    j0 = cols_ref[2 * h, first + r] - base
                    j1 = cols_ref[2 * h + 1, first + r] - base
                    right = jnp.concatenate(
                        [
                            jnp.concatenate([table[j0], zero], axis=1),
                            jnp.concatenate([zero, table[j1]], axis=1),
                        ],
                        axis=0,
                    )
                    products.append(
                        jnp.dot(
                            a_buf[first + r, :, 128 * h:128 * h + 128], right,
                            preferred_element_type=F32,
                        ).astype(BF)
                    )
            pieces = []
            for r in range(group):
                i = first + r
                pt = left[i // 2, pl.ds(pl.multiple_of(64 * (r % 2), 64), 64), :]
                for h in range(2):
                    pieces.append(jnp.dot(pt, products[2 * r + h], preferred_element_type=F32))
            for r in range(group):
                i = first + r
                a = smaps[2, i]
                for s in range(4):
                    j = cols_ref[s, i] - base
                    b = smaps[j // 128, j % 128]
                    at = pl.multiple_of(((b // 2) * 16 + a) * 64, 64)
                    acc[pl.ds(at, 64), :] += pieces[2 * r + s // 2][:, 128 * (s % 2):128 * (s % 2) + 128]

    for d in range(ROWS):
        out_buf[d] = acc[pl.ds(1024 * d, 1024), :].astype(BF)
        pltpu.make_async_copy(out_buf.at[d], out_hbm.at[d], out_sem.at[d]).start()
    for d in range(ROWS):
        pltpu.make_async_copy(out_buf.at[d], out_hbm.at[d], out_sem.at[d]).wait()


def blocks(a_cols, a_rows, col_p, row_p):
    smem = pl.BlockSpec(memory_space=pltpu.SMEM)
    vmem = pl.BlockSpec(memory_space=pltpu.VMEM)
    hbm = pl.BlockSpec(memory_space=pl.ANY)
    return pl.pallas_call(
        blocks_kernel,
        out_shape=jax.ShapeDtypeStruct((ROWS, 1024, 128), BF),
        in_specs=[smem, hbm, vmem, vmem],
        out_specs=hbm,
        scratch_shapes=[
            pltpu.VMEM((128, 64, 256), BF),
            pltpu.VMEM((256, 64, 128), BF),
            pltpu.VMEM((64, 128, 64), BF),
            pltpu.VMEM((ROWS * 1024, 128), F32),
            pltpu.VMEM((ROWS, 1024, 128), BF),
            pltpu.VMEM((8, 128), jnp.int32),
            pltpu.SMEM((8, 128), jnp.int32),
            pltpu.SemaphoreType.DMA((128 // CHUNK,)),
            pltpu.SemaphoreType.DMA((ROWS,)),
            pltpu.SemaphoreType.DMA,
        ],
        compiler_params=pltpu.CompilerParams(vmem_limit_bytes=32 * MIB),
    )(a_cols, a_rows, col_p, row_p)


def exchange_kernel(src_ref, out_ref, send_sem, recv_sem, local_sem):
    row = lax.axis_index("row")
    col = lax.axis_index("col")
    barrier = pltpu.get_barrier_semaphore()

    @pl.loop(1, ROWS)
    def _(step):
        pl.semaphore_signal(barrier, 1, device_id=((row + step) % ROWS, col), device_id_type=MESH)

    pl.semaphore_wait(barrier, ROWS - 1)
    own = pltpu.make_async_copy(src_ref.at[row], out_ref.at[row], local_sem)
    own.start()

    def copy(step):
        to = (row + step) % ROWS
        return pltpu.make_async_remote_copy(
            src_ref=src_ref.at[to],
            dst_ref=out_ref.at[row],
            send_sem=send_sem.at[step],
            recv_sem=recv_sem.at[row],
            device_id=(to, col),
            device_id_type=MESH,
        )

    @pl.loop(1, ROWS)
    def _(step):
        copy(step).start()

    own.wait()

    @pl.loop(1, ROWS)
    def _(step):
        copy(step).wait_send()
        src = (row + step) % ROWS
        pltpu.make_async_copy(out_ref.at[src], out_ref.at[src], recv_sem.at[src]).wait()


def exchange(parts):
    return pl.pallas_call(
        exchange_kernel,
        out_shape=jax.ShapeDtypeStruct(parts.shape, parts.dtype),
        in_specs=[pl.BlockSpec(memory_space=pl.ANY)],
        out_specs=pl.BlockSpec(memory_space=pl.ANY),
        scratch_shapes=[
            pltpu.SemaphoreType.DMA((ROWS,)),
            pltpu.SemaphoreType.DMA((ROWS,)),
            pltpu.SemaphoreType.DMA,
        ],
        compiler_params=pltpu.CompilerParams(
            collective_id=1, has_side_effects=True, vmem_limit_bytes=MIB
        ),
    )(parts)


def per_device(a_tiles, a_cols, p_tiles, agg_sizes):
    col_p, row_p, a_rows = spread(p_tiles, agg_sizes, a_tiles.transpose(1, 2, 3, 0))
    parts = blocks(a_cols.T, a_rows, col_p, row_p)
    got = exchange(parts)
    return got.reshape(256, 64, 128).astype(F32)


def solution(mesh):
    return jax.shard_map(
        per_device,
        mesh=mesh,
        in_specs=(
            P("row", "col", None, None),
            P("row", "col"),
            P(("col", "row"), None, None),
            P("row", None),
        ),
        out_specs=P(None, None, ("col", "row")),
        check_vma=False,
    )
```

time: 193 us -> 139 us (0.72)
  the two profiles are of different devices: /device:TPU:5 before, /device:TPU:1 now
where the time goes in v1:
time: 139 us
  Pallas kernels  130 us (94%)
  other arithmetic  4.43 us (3%)
  local copies, waits for them, and re-layouts  3.81 us (3%)
    pallas_call x1, Pallas kernels, exchange(): pl.pallas_call(exchange_kernel, out_shape=jax.ShapeDtypeStruct(parts.shap...  76.4 us
    pallas_call x1, Pallas kernels, spread(): pl.pallas_call(spread_kernel, out_shape=(jax.ShapeDtypeStruct((ROWS, 528,...  28.2 us
    pallas_call x1, Pallas kernels, blocks(): pl.pallas_call(blocks_kernel, out_shape=jax.ShapeDtypeStruct((ROWS, 1024,...  25.6 us
    convert_element_type x1, other arithmetic, per_device(): return got.reshape(256, 64, 128).astype(F32)  4.43 us
    unnamed x8, local copies, waits for them, and re-layouts  3.81 us

profile of v1, /device:TPU:1, one launch (start us, length us, event | category | flops | bytes accessed | tf_op | source)
XLA Modules:
  0.0 138.6 jit_solution(808761093215045806)
XLA Ops:
  0.0 0.0 copy-start.2
  0.0 0.0 copy-start
  0.0 2.2 %copy-done = bf16[128,4,64,64]{0,3,2,1:T(8,128)(2,1)S(1)} copy-done((bf16[128,4,64,64]{0,3,2,1:T(8,128)(2,1)S(1)}, bf16[128,4,64,64]{0,3,2,1:T(8,128)(2,1)}, u32[]{:S(2)}) %copy-start) | copy-done | bytes 4194328
  2.2 0.0 copy-start.1
  2.2 0.9 copy-done.1
  3.2 0.0 copy-start.3
  3.2 0.7 copy-done.3
  3.8 28.2 %shard_map.46 = (bf16[16,528,128]{2,1,0:T(8,128)(2,1)S(1)}, bf16[8,512,128]{2,1,0:T(8,128)(2,1)S(1)}, bf16[128,64,256]{2,1,0:T(8,128)(2,1)S(1)}) custom-call(bf16[16,64,64]{2,1,0:T(8,128)(2,1)S(1)} %copy-done.1, s32[1,16]{1,0:T(1,128)S(1)} %copy-done.3, bf16[4,64,64,128]{3,2,1,0:T(8,128)(2,1)S(1)} %bitcast.5), custom_call_target="tpu_custom_call" | custom-call | tf_op jit(solution)/shard_map/pallas_call | solution.py:196
  32.0 0.0 copy-done.2
  32.0 25.6 %shard_map.47.src_ref = bf16[16,1024,128]{2,1,0:T(8,128)(2,1)S(1)} custom-call(s32[4,128]{1,0:T(4,128)S(1)} %bitcast.6, bf16[128,64,256]{2,1,0:T(8,128)(2,1)S(1)} %get-tuple-element.8.a_hbm, bf16[16,528,128]{2,1,0:T(8,128)(2,1)S(1)} %get-tuple-element.9.col_ref, bf16[8,512,128]{2,1,0:T(8,128)(2,1)S(1)} %get-tuple-element.10.row_ref), custom_call_target="tpu_custom_call" | custom-call | tf_op jit(solution)/shard_map/pallas_call | solution.py:337
  57.7 76.4 %shard_map.48 = bf16[16,1024,128]{2,1,0:T(8,128)(2,1)S(1)} custom-call(bf16[16,1024,128]{2,1,0:T(8,128)(2,1)S(1)} %shard_map.47.src_ref), custom_call_target="tpu_custom_call" | custom-call | tf_op jit(solution)/shard_map/pallas_call | solution.py:396
  134.1 4.4 %convert.1 = f32[256,64,128]{2,1,0:T(8,128)} convert(bf16[256,64,128]{2,1,0:T(8,128)(2,1)S(1)} %bitcast.4) | non-fusion elementwise | flops 2097152 | bytes 12582912 | tf_op jit(solution)/shard_map/convert_element_type | solution.py:416
Async XLA Ops:
  0.0 32.0 %copy-start.2 = (s32[128,4]{0,1:T(4,128)S(1)}, s32[128,4]{0,1:T(4,128)}, u32[]{:S(2)}) copy-start(s32[128,4]{0,1:T(4,128)} %param.5) | copy-start | bytes 6148
  0.0 2.2 %copy-start = (bf16[128,4,64,64]{0,3,2,1:T(8,128)(2,1)S(1)}, bf16[128,4,64,64]{0,3,2,1:T(8,128)(2,1)}, u32[]{:S(2)}) copy-start(bf16[128,4,64,64]{0,3,2,1:T(8,128)(2,1)} %param.4) | copy-start | bytes 12582916
  2.2 0.9 copy-start.1
  3.2 0.7 copy-start.3
